TPU v7x, 256 devices: a whole 4x4x8 slice. The times are simulated.
256 devices in a mesh: energy: 64 (over y, z, x_hi), slab: 4 (over x_lo, core).
Axes of the slice: x: 4 (x_hi: 2, x_lo: 2; x = x_hi * 2 + x_lo), y: 4, z: 8, core: 2. Of those that a mesh axis runs over, the one named last changes fastest.
Arguments:
- lesser: bfloat16 [64, 4, 2, 1024, 1024], P('energy', 'slab'), may hold values from -6 to 6
- greater_diag: float32 [64, 4, 1024], P('energy', 'slab'), may hold values from -6 to 6
- dipole: bfloat16 [4, 1024, 1024], P('slab'), may hold values from -0.1875 to 0.1875
- photon_weights: float32 [64, 3], P('energy'), may hold values from 0.2 to 1
- sidebands: int32 [64], P('energy'), may hold values from 1 to 2
- phonon_lags: int32 [6], replicated, may hold values from 1 to 31
- phonon_strengths: float32 [2, 6], replicated, may hold values from 0.3 to 1.5
- slab_coupling: float32 [4, 1024], P('slab'), may hold values from 0.3 to 1
Outputs:
- lesser_self: bfloat16 [64, 4, 2, 1024, 1024], P('energy', 'slab')
- greater_phonon: float32 [64, 4, 1024], P('energy', 'slab')
All inputs are finite; a program needn't handle non-finite values.
Results may differ from a plain program's by a relative error of at most 0.0057.
Values may be sent and summed in bfloat16 or wider, within the bound.
A program may use at most 64 MiB of HBM per device.

v0:
```python
import jax
import jax.numpy as jnp
from jax import lax
from jax.sharding import PartitionSpec as P

PHOT_BLOCKS = 3


def extended(block, sides, width):
    for axis, dim in sides:
        count = lax.axis_size(axis)
        forward = [(i, i + 1) for i in range(count - 1)]
        backward = [(target, source) for source, target in forward]
        low = lax.ppermute(
            lax.slice_in_dim(block, block.shape[dim] - width, None, axis=dim), axis, forward
        )
        high = lax.ppermute(lax.slice_in_dim(block, 0, width, axis=dim), axis, backward)
        block = jnp.concatenate([low, block, high], axis=dim)
    return block


def shifted(block, axis, distance):
    devices = range(lax.axis_size(axis))
    route = [(i - distance, i) for i in devices if i - distance in devices]
    return lax.ppermute(block, axis, route)


def kernel(rows, cols, phonon_lags, first, second):
    offset = cols[None, :] - rows[:, None]
    upward = (offset[None, :, :] == phonon_lags[:, None, None]).astype(jnp.float32)
    downward = (offset[None, :, :] == -phonon_lags[:, None, None]).astype(jnp.float32)
    return jnp.sum(first[:, None, None] * upward + second[:, None, None] * downward, axis=0)


def left_of(blocks, dipole):
    return jnp.einsum(
        "escij,skj->escik", blocks, dipole, preferred_element_type=jnp.float32
    ).astype(jnp.bfloat16)


def on_device(
    lesser,
    greater_diag,
    dipole,
    photon_weights,
    sidebands,
    phonon_lags,
    phonon_strengths,
    slab_coupling,
):
    e_count = lesser.shape[0]
    width = lesser.shape[-1]
    total_e = e_count * lax.axis_size("energy")
    own_rows = lax.axis_index("energy") * e_count + jnp.arange(e_count, dtype=jnp.int32)
    diag_less = jnp.diagonal(lesser[:, :, 1], axis1=-2, axis2=-1).astype(jnp.float32)
    stacked_diag = jnp.concatenate([diag_less, greater_diag], axis=-1)
    everyone = lax.all_gather(stacked_diag, "energy", axis=0, tiled=True)
    all_rows = jnp.arange(total_e, dtype=jnp.int32)
    k_less = kernel(own_rows, all_rows, phonon_lags, phonon_strengths[0], phonon_strengths[1])
    k_great = kernel(own_rows, all_rows, phonon_lags, phonon_strengths[1], phonon_strengths[0])
    corr_less = jnp.einsum(
        "ef,fsn->esn", k_less, everyone[..., :width], precision=lax.Precision.HIGHEST
    )
    corr_great = jnp.einsum(
        "ef,fsn->esn", k_great, everyone[..., width:], precision=lax.Precision.HIGHEST
    )
    correlated = jnp.concatenate([corr_less, corr_great], axis=-1)
    coupling = jnp.concatenate([slab_coupling, slab_coupling], axis=-1)
    outgoing = jnp.stack([correlated, coupling * correlated])
    rims = extended(outgoing, (("slab", 2),), 1)
    phonon = correlated + rims[1, :, 0:1] + coupling * rims[0, :, 2:3]
    own_left = left_of(lesser, dipole)
    lower = shifted(own_left, "energy", PHOT_BLOCKS)
    upper = shifted(own_left, "energy", -PHOT_BLOCKS)
    weights = photon_weights[:, :, None, None, None, None]
    flags = sidebands.astype(jnp.float32)[:, None, None, None, None]
    mixed = (
        weights[:, 0] * own_left.astype(jnp.float32)
        + flags
        * (weights[:, 1] * lower.astype(jnp.float32) + weights[:, 2] * upper.astype(jnp.float32))
    ).astype(jnp.bfloat16)
    photon = jnp.einsum("sij,escjk->escik", dipole, mixed, preferred_element_type=jnp.float32)
    eye_mask = (jnp.arange(width)[:, None] == jnp.arange(width)[None, :]).astype(jnp.float32)
    photon = photon.at[:, :, 1].add(eye_mask * phonon[..., :width, None])
    return (photon.astype(jnp.bfloat16), phonon[..., width:])


def solution(mesh):
    return jax.shard_map(
        on_device,
        mesh=mesh,
        in_specs=(
            P("energy", "slab", None, None, None),
            P("energy", "slab", None),
            P("slab", None, None),
            P("energy", None),
            P("energy"),
            P(),
            P(),
            P("slab", None),
        ),
        out_specs=(P("energy", "slab", None, None, None), P("energy", "slab", None)),
        check_vma=False,
    )
```

profile of v0, /device:TPU:1, one launch (start us, length us, event | category | flops | bytes accessed | tf_op | source)
XLA Modules:
  0.0 408.2 jit_solution(17339647209610599391)
XLA Ops:
  0.6 0.0 copy-start
  0.6 0.0 copy-start.5
  0.7 1.6 copy-done
  2.2 8.3 %convert_bitcast_fusion = bf16[1,1,2,1024,1024]{3,4,2,0,1:T(8,128)(2,1)} fusion(bf16[1,1,2,1024,1024]{4,3,2,1,0:T(8,128)(2,1)} %param.10, bf16[1,1024,1024]{2,1,0:T(8,128)(2,1)S(1)} %copy-done), kind=kOutput, calls=%fused_computation.13 | convolution fusion | flops 4297064448 | bytes 10485760 | tf_op jit(solution)/shard_map/escij,skj->escik/dot_general | solution.py:36
  10.5 0.0 copy-start.1
  10.5 0.0 copy-start.4
  10.5 0.0 copy-start.3
  10.5 1.4 collective-permute-start.1
  11.9 9.4 %collective-permute-start = (bf16[1,1,2,1024,1024]{3,4,2,0,1:T(8,128)(2,1)}, bf16[1,1,2,1024,1024]{3,4,2,0,1:T(8,128)(2,1)}, u32[]{:S(2)}, u32[]{:S(2)}) collective-permute-start(bf16[1,1,2,1024,1024]{3,4,2,0,1:T(8,128)(2,1)} %convert_bitcast_fusion), channel_id=1, source_target_pairs={{0,12},{4,16},{8,20},{12,24},{16,28},{20,32},{24,36},{28,40},{32,4... | collective-permute-start | bytes 12582920 | tf_op jit(solution)/shard_map/ppermute | solution.py:25
  21.4 0.0 copy-done.5
  21.4 0.0 copy-start.2
  21.4 3.1 slice_bitcast_fusion.1
  24.5 16.3 %gather_fusion = bf16[1024]{0:T(1024)(128)(2,1)S(1)} fusion(bf16[1024,1024]{1,0:T(8,128)(2,1)} %slice_bitcast_fusion.1, s32[1024]{0:T(1024)S(1)} %bitcast.83), kind=kCustom, calls=%fused_computation | custom fusion | bytes 12288 | tf_op jit(solution)/shard_map/jit(diagonal)/gather | solution.py:55
  40.8 0.0 copy-done.1
  40.9 0.0 copy-done.4
  40.9 0.1 fusion.27
  41.0 0.0 copy-done.3
  41.0 305.5 %all_gather.3 = f32[64,1,2048]{2,1,0:T(1,128)S(1)} all-gather(f32[1,1,2048]{2,1,0:T(1,128)S(1)} %pad_maximum_fusion.1), channel_id=1, replica_groups=mesh['energy'=64,'slab'=4] {'energy'}, dimensions={0}, use_global_device_ids=true | all-gather | bytes 532480 | tf_op jit(solution)/shard_map/all_gather | solution.py:57
  346.6 0.3 fusion.18
  346.8 0.3 fusion.15
  347.2 35.3 %collective-permute-start.3 = (f32[2,1,1,2048]{3,2,1,0:T(1,128)S(1)}, f32[2,1,1,2048]{3,2,1,0:T(1,128)S(1)}, u32[]{:S(2)}, u32[]{:S(2)}) collective-permute-start(f32[2,1,1,2048]{3,2,1,0:T(1,128)S(1)} %pad_maximum_fusion), channel_id=1, source_target_pairs={{1,0},{2,1},{3,2},{5,4},{6,5},{7,6},{9,8},{10,9},{11,10},{13,12},{... | collective-permute-start | bytes 49160 | tf_op jit(solution)/shard_map/ppermute | solution.py:17
  382.5 2.6 collective-permute-start.2
  385.1 0.0 copy-done.2
  385.2 0.6 fusion.33
  386.4 0.0 collective-permute-done.3
  386.5 0.0 collective-permute-done.2
  386.5 0.6 fusion.32
  387.1 0.0 collective-permute-done.1
  387.1 0.0 collective-permute-done
  387.1 10.0 %fusion.1 = f32[2,1024,1024]{2,1,0:T(8,128)S(1)} fusion(bf16[1,1,2,1024,1024]{3,4,2,0,1:T(8,128)(2,1)} %collective-permute-done.1, bf16[1,1,2,1024,1024]{3,4,2,0,1:T(8,128)(2,1)} %collective-permute-done, bf16[1,1,2,1024,1024]{3,4,2,0,1:T(8,128)(2,1)} %convert_bitcast_fusion, f32[]{:T(128)} %bitcast.10, f32[]{:T(128)} %bitcast.8, f32[]{:T(128)} %bitcast.7, ...), kind=kOutput, calls=%fused_computation.3 | convolution fusion | flops 4315938816 | bytes 23068688 | tf_op jit(solution)/shard_map/sij,escjk->escik/dot_general | solution.py:82
  397.1 1.7 copy.25
  398.7 0.7 fusion.4
  399.4 2.6 convert_element_type.53
  402.0 6.2 %copy.13 = bf16[1,1,2,1024,1024]{4,3,2,1,0:T(8,128)(2,1)} copy(bf16[1,1,2,1024,1024]{3,4,2,0,1:T(8,128)(2,1)} %convert_element_type.53) | data formatting | bytes 8388608
  (13 shorter events, 0.2 us)
Async XLA Ops:
  0.6 1.6 copy-start
  0.6 20.7 %copy-start.5 = (s32[6]{0:T(128)S(1)}, s32[6]{0:T(128)}, u32[]{:S(2)}) copy-start(s32[6]{0:T(128)} %param.15) | copy-start | bytes 76
  10.5 30.4 %copy-start.1 = (f32[1,1024]{1,0:T(1,128)S(1)}, f32[1,1024]{1,0:T(1,128)}, u32[]{:S(2)}) copy-start(f32[1,1024]{1,0:T(1,128)} %param.17) | copy-start | bytes 12292
  10.5 30.4 %copy-start.4 = (f32[2,6]{1,0:T(2,128)S(1)}, f32[2,6]{1,0:T(2,128)}, u32[]{:S(2)}) copy-start(f32[2,6]{1,0:T(2,128)} %param.16) | copy-start | bytes 148
  10.5 30.5 %copy-start.3 = (f32[1,1,1024]{2,1,0:T(1,128)S(1)}, f32[1,1,1024]{2,1,0:T(1,128)}, u32[]{:S(2)}) copy-start(f32[1,1,1024]{2,1,0:T(1,128)} %param.11) | copy-start | bytes 12292
  10.5 376.6 %collective-permute-start.1 = (bf16[1,1,2,1024,1024]{3,4,2,0,1:T(8,128)(2,1)}, bf16[1,1,2,1024,1024]{3,4,2,0,1:T(8,128)(2,1)}, u32[]{:S(2)}, u32[]{:S(2)}) collective-permute-start(bf16[1,1,2,1024,1024]{3,4,2,0,1:T(8,128)(2,1)} %convert_bitcast_fusion), channel_id=1, source_target_pairs={{12,0},{16,4},{20,8},{24,12},{28,16},{32,20},{36,24},{40,28},{44,3... | collective-permute-start | bytes 12582920 | tf_op jit(solution)/shard_map/ppermute | solution.py:25
  11.9 375.2 %collective-permute-start = (bf16[1,1,2,1024,1024]{3,4,2,0,1:T(8,128)(2,1)}, bf16[1,1,2,1024,1024]{3,4,2,0,1:T(8,128)(2,1)}, u32[]{:S(2)}, u32[]{:S(2)}) collective-permute-start(bf16[1,1,2,1024,1024]{3,4,2,0,1:T(8,128)(2,1)} %convert_bitcast_fusion), channel_id=1, source_target_pairs={{0,12},{4,16},{8,20},{12,24},{16,28},{20,32},{24,36},{28,40},{32,4... | collective-permute-start | bytes 12582920 | tf_op jit(solution)/shard_map/ppermute | solution.py:25
  21.4 363.8 %copy-start.2 = (f32[1,3]{1,0:T(1,128)S(1)}, f32[1,3]{1,0:T(1,128)}, u32[]{:S(2)}) copy-start(f32[1,3]{1,0:T(1,128)} %param.13) | copy-start | bytes 40
  347.2 39.3 %collective-permute-start.3 = (f32[2,1,1,2048]{3,2,1,0:T(1,128)S(1)}, f32[2,1,1,2048]{3,2,1,0:T(1,128)S(1)}, u32[]{:S(2)}, u32[]{:S(2)}) collective-permute-start(f32[2,1,1,2048]{3,2,1,0:T(1,128)S(1)} %pad_maximum_fusion), channel_id=1, source_target_pairs={{1,0},{2,1},{3,2},{5,4},{6,5},{7,6},{9,8},{10,9},{11,10},{13,12},{... | collective-permute-start | bytes 49160 | tf_op jit(solution)/shard_map/ppermute | solution.py:17
  382.5 4.0 collective-permute-start.2
where the time goes:
time: 409 us; the launch traced here: 408 us
  blocking collectives  306 us (75%)
  starting transfers between devices  48.8 us (12%)
  local copies, waits for them, and re-layouts  30.2 us (7%)
  matrix products  18.8 us (5%)
    all_gather x1, blocking collectives, on_device(): everyone = lax.all_gather(stacked_diag, 'energy', axis=0, tiled=True)  306 us
    ppermute x1, starting transfers between devices, extended(): lax.ppermute(lax.slice_in_dim(block, 0, width, axis=dim), axis, backward)  35.3 us
    gather x1, local copies, waits for them, and re-layouts, on_device(): jnp.diagonal(lesser[:, :, 1], axis1=-2, axis2=-1).astype(jnp.float32)  16.3 us
    ppermute x2, starting transfers between devices, shifted(): return lax.ppermute(block, axis, route)  10.9 us
    dot_general x1, matrix products, on_device(): jnp.einsum('sij,escjk->escik', dipole, mixed, preferred_element_type=jnp....  9.97 us
    unnamed x15, local copies, waits for them, and re-layouts  9.44 us
    dot_general x1, matrix products, left_of(): jnp.einsum('escij,skj->escik', blocks, dipole, preferred_element_type=jnp...  8.26 us
  transfers between devices with their start and end apart: 4, of which 0 were waited for; matrix products, arithmetic and copies ran while one was open for 5% of the time, Pallas kernels for 0%

commit v1 on v0

--- a/solution.py
+++ b/solution.py
@@ -54,7 +54,8 @@
     own_rows = lax.axis_index("energy") * e_count + jnp.arange(e_count, dtype=jnp.int32)
     diag_less = jnp.diagonal(lesser[:, :, 1], axis1=-2, axis2=-1).astype(jnp.float32)
     stacked_diag = jnp.concatenate([diag_less, greater_diag], axis=-1)
-    everyone = lax.all_gather(stacked_diag, "energy", axis=0, tiled=True)
+    repeated = jnp.stack([stacked_diag] * lax.axis_size("energy"))
+    everyone = jnp.concatenate(lax.all_to_all(repeated, "energy", 0, 0), axis=0)
     all_rows = jnp.arange(total_e, dtype=jnp.int32)
     k_less = kernel(own_rows, all_rows, phonon_lags, phonon_strengths[0], phonon_strengths[1])
     k_great = kernel(own_rows, all_rows, phonon_lags, phonon_strengths[1], phonon_strengths[0])

time: 409 us -> 255 us (0.62)
  blocking collectives: 306 us -> 0 us
  waiting for transfers between devices: 0.01 us -> 170 us
  starting transfers between devices: 48.8 us -> 30.7 us
    all_gather x1 -> x0, blocking collectives: 306 us -> none  [on_device(): everyone = lax.all_gather(stacked_diag, 'energy', axis=0, tiled=True)]
    all_to_all x0 -> x1, waiting for transfers between devices: none -> 170 us  [on_device(): everyone = jnp.concatenate(lax.all_to_all(repeated, 'energy', 0, 0), axis=0)]
    ppermute x1, starting transfers between devices: 35.3 us -> 3.42 us  [extended(): lax.ppermute(lax.slice_in_dim(block, 0, width, axis=dim), axis, backward)]
    all_to_all x0 -> x1, starting transfers between devices: none -> 14.3 us  [on_device(): everyone = jnp.concatenate(lax.all_to_all(repeated, 'energy', 0, 0), axis=0)]
    unnamed x15 -> x17, local copies, waits for them, and re-layouts: 9.44 us -> 9.45 us
  transfers between devices with their start and end apart: 4 -> 5, of which waited for: 0 -> 1; matrix products, arithmetic and copies ran while one was open for 5% -> 8% of each run, Pallas kernels for 0% -> 0%
where the time goes in v1:
time: 255 us; the launch traced here: 254 us
  waiting for transfers between devices  170 us (67%)
  starting transfers between devices  30.7 us (12%)
  local copies, waits for them, and re-layouts  29.6 us (12%)
  matrix products  19 us (7%)
  other arithmetic  3.5 us (1%)
    all_to_all x1, waiting for transfers between devices, on_device(): everyone = jnp.concatenate(lax.all_to_all(repeated, 'energy', 0, 0), axis=0)  170 us
    gather x1, local copies, waits for them, and re-layouts, on_device(): jnp.diagonal(lesser[:, :, 1], axis1=-2, axis2=-1).astype(jnp.float32)  16.2 us
    all_to_all x1, starting transfers between devices, on_device(): everyone = jnp.concatenate(lax.all_to_all(repeated, 'energy', 0, 0), axis=0)  14.3 us
    ppermute x2, starting transfers between devices, shifted(): return lax.ppermute(block, axis, route)  10.8 us
    dot_general x1, matrix products, on_device(): jnp.einsum('sij,escjk->escik', dipole, mixed, preferred_element_type=jnp....  9.96 us
    unnamed x17, local copies, waits for them, and re-layouts  9.45 us
    dot_general x1, matrix products, left_of(): jnp.einsum('escij,skj->escik', blocks, dipole, preferred_element_type=jnp...  8.51 us
  transfers between devices with their start and end apart: 5, of which 1 were waited for; matrix products, arithmetic and copies ran while one was open for 8% of the time, Pallas kernels for 0%

profile of v1, /device:TPU:1, one launch (start us, length us, event | category | flops | bytes accessed | tf_op | source)
XLA Modules:
  0.0 254.1 jit_solution(8168668929240933080)
XLA Ops:
  0.6 0.0 copy-start
  0.6 0.0 copy-start.1
  0.7 1.6 copy-done
  2.2 8.5 %convert_bitcast_fusion = bf16[1,1,2,1024,1024]{3,4,2,0,1:T(8,128)(2,1)} fusion(bf16[1,1,2,1024,1024]{4,3,2,1,0:T(8,128)(2,1)} %param.10, bf16[1,1024,1024]{2,1,0:T(8,128)(2,1)S(1)} %copy-done), kind=kOutput, calls=%fused_computation.13 | convolution fusion | flops 4297064448 | bytes 10485760 | tf_op jit(solution)/shard_map/escij,skj->escik/dot_general | solution.py:36
  10.7 0.0 copy-start.4
  10.7 1.4 collective-permute-start.1
  12.2 9.4 %collective-permute-start = (bf16[1,1,2,1024,1024]{3,4,2,0,1:T(8,128)(2,1)}, bf16[1,1,2,1024,1024]{3,4,2,0,1:T(8,128)(2,1)}, u32[]{:S(2)}, u32[]{:S(2)}) collective-permute-start(bf16[1,1,2,1024,1024]{3,4,2,0,1:T(8,128)(2,1)} %convert_bitcast_fusion), channel_id=1, source_target_pairs={{0,12},{4,16},{8,20},{12,24},{16,28},{20,32},{24,36},{28,40},{32,4... | collective-permute-start | bytes 12582920 | tf_op jit(solution)/shard_map/ppermute | solution.py:25
  21.6 0.0 copy-done.1
  21.6 0.0 copy-start.6
  21.6 0.0 copy-start.2
  21.6 0.0 copy-start.5
  21.6 0.0 copy-start.3
  21.6 1.5 slice_bitcast_fusion.1
  23.2 16.2 %gather_fusion = bf16[1024]{0:T(1024)(128)(2,1)S(1)} fusion(bf16[1024,1024]{1,0:T(8,128)(2,1)} %slice_bitcast_fusion.1, s32[1024]{0:T(1024)S(1)} %bitcast.85), kind=kCustom, calls=%fused_computation | custom fusion | bytes 12288 | tf_op jit(solution)/shard_map/jit(diagonal)/gather | solution.py:55
  39.4 0.0 copy-done.4
  39.5 1.1 stack.6
  40.5 14.3 %all-to-all-start = ((f32[64,1,1,2048]{3,2,1,0:T(1,128)}), f32[64,1,1,2048]{3,2,1,0:T(1,128)S(1)}, u32[]{:S(2)}, u32[]{:S(2)}) async-start(f32[64,1,1,2048]{3,2,1,0:T(1,128)} %stack.6), calls=%async_computation | async-start | bytes 1048576 | tf_op jit(solution)/shard_map/all_to_all | solution.py:58
  54.9 0.0 copy-done.6
  54.9 0.0 copy-done.2
  54.9 0.0 copy-done.5
  55.0 0.1 fusion.27
  55.1 169.7 %all-to-all-done = f32[64,1,1,2048]{3,2,1,0:T(1,128)S(1)} async-done(((f32[64,1,1,2048]{3,2,1,0:T(1,128)}), f32[64,1,1,2048]{3,2,1,0:T(1,128)S(1)}, u32[]{:S(2)}, u32[]{:S(2)}) %all-to-all-start) | async-done | bytes 524320 | tf_op jit(solution)/shard_map/all_to_all | solution.py:58
  224.8 0.3 fusion.18
  225.1 0.3 fusion.15
  225.5 3.4 %collective-permute-start.3 = (f32[2,1,1,2048]{3,2,1,0:T(1,128)S(1)}, f32[2,1,1,2048]{3,2,1,0:T(1,128)S(1)}, u32[]{:S(2)}, u32[]{:S(2)}) collective-permute-start(f32[2,1,1,2048]{3,2,1,0:T(1,128)S(1)} %pad_maximum_fusion), channel_id=1, source_target_pairs={{1,0},{2,1},{3,2},{5,4},{6,5},{7,6},{9,8},{10,9},{11,10},{13,12},{... | collective-permute-start | bytes 49160 | tf_op jit(solution)/shard_map/ppermute | solution.py:17
  228.9 2.1 collective-permute-start.2
  231.0 0.0 copy-done.3
  231.0 0.6 fusion.33
  232.3 0.0 collective-permute-done.3
  232.4 0.0 collective-permute-done.2
  232.4 0.6 fusion.32
  233.0 0.0 collective-permute-done.1
  233.0 0.0 collective-permute-done
  233.0 10.0 %fusion.1 = f32[2,1024,1024]{2,1,0:T(8,128)S(1)} fusion(bf16[1,1,2,1024,1024]{3,4,2,0,1:T(8,128)(2,1)} %collective-permute-done.1, bf16[1,1,2,1024,1024]{3,4,2,0,1:T(8,128)(2,1)} %collective-permute-done, bf16[1,1,2,1024,1024]{3,4,2,0,1:T(8,128)(2,1)} %convert_bitcast_fusion, f32[]{:T(128)} %bitcast.10, f32[]{:T(128)} %bitcast.8, f32[]{:T(128)} %bitcast.7, ...), kind=kOutput, calls=%fused_computation.3 | convolution fusion | flops 4315938816 | bytes 23068688 | tf_op jit(solution)/shard_map/sij,escjk->escik/dot_general | solution.py:83
  243.0 1.7 copy.24
  244.6 0.7 fusion.4
  245.3 2.6 %convert_element_type.53 = bf16[1,1,2,1024,1024]{3,4,2,0,1:T(8,128)(2,1)} convert(f32[1,1,2,1024,1024]{3,4,2,0,1:T(8,128)S(1)} %fusion.4) | non-fusion elementwise | flops 2097152 | bytes 12582912 | tf_op jit(solution)/shard_map/convert_element_type | solution.py:86
  247.9 6.2 %copy.12 = bf16[1,1,2,1024,1024]{4,3,2,1,0:T(8,128)(2,1)} copy(bf16[1,1,2,1024,1024]{3,4,2,0,1:T(8,128)(2,1)} %convert_element_type.53) | data formatting | bytes 8388608
  (13 shorter events, 0.2 us)
Async XLA Ops:
  0.6 1.6 copy-start
  0.6 21.0 %copy-start.1 = (bf16[1,1,2,1024,1024]{4,3,2,1,0:T(8,128)(2,1)S(1)}, bf16[1,1,2,1024,1024]{4,3,2,1,0:T(8,128)(2,1)}, u32[]{:S(2)}) copy-start(bf16[1,1,2,1024,1024]{4,3,2,1,0:T(8,128)(2,1)} %param.10) | copy-start | bytes 12582916
  10.7 28.7 %copy-start.4 = (f32[1,1,1024]{2,1,0:T(1,128)S(1)}, f32[1,1,1024]{2,1,0:T(1,128)}, u32[]{:S(2)}) copy-start(f32[1,1,1024]{2,1,0:T(1,128)} %param.11) | copy-start | bytes 12292
  10.7 222.3 %collective-permute-start.1 = (bf16[1,1,2,1024,1024]{3,4,2,0,1:T(8,128)(2,1)}, bf16[1,1,2,1024,1024]{3,4,2,0,1:T(8,128)(2,1)}, u32[]{:S(2)}, u32[]{:S(2)}) collective-permute-start(bf16[1,1,2,1024,1024]{3,4,2,0,1:T(8,128)(2,1)} %convert_bitcast_fusion), channel_id=1, source_target_pairs={{12,0},{16,4},{20,8},{24,12},{28,16},{32,20},{36,24},{40,28},{44,3... | collective-permute-start | bytes 12582920 | tf_op jit(solution)/shard_map/ppermute | solution.py:25
  12.2 220.8 %collective-permute-start = (bf16[1,1,2,1024,1024]{3,4,2,0,1:T(8,128)(2,1)}, bf16[1,1,2,1024,1024]{3,4,2,0,1:T(8,128)(2,1)}, u32[]{:S(2)}, u32[]{:S(2)}) collective-permute-start(bf16[1,1,2,1024,1024]{3,4,2,0,1:T(8,128)(2,1)} %convert_bitcast_fusion), channel_id=1, source_target_pairs={{0,12},{4,16},{8,20},{12,24},{16,28},{20,32},{24,36},{28,40},{32,4... | collective-permute-start | bytes 12582920 | tf_op jit(solution)/shard_map/ppermute | solution.py:25
  21.6 33.3 %copy-start.6 = (s32[6]{0:T(128)S(1)}, s32[6]{0:T(128)}, u32[]{:S(2)}) copy-start(s32[6]{0:T(128)} %param.15) | copy-start | bytes 76
  21.6 33.3 %copy-start.2 = (f32[1,1024]{1,0:T(1,128)S(1)}, f32[1,1024]{1,0:T(1,128)}, u32[]{:S(2)}) copy-start(f32[1,1024]{1,0:T(1,128)} %param.17) | copy-start | bytes 12292
  21.6 33.3 %copy-start.5 = (f32[2,6]{1,0:T(2,128)S(1)}, f32[2,6]{1,0:T(2,128)}, u32[]{:S(2)}) copy-start(f32[2,6]{1,0:T(2,128)} %param.16) | copy-start | bytes 148
  21.6 209.4 %copy-start.3 = (f32[1,3]{1,0:T(1,128)S(1)}, f32[1,3]{1,0:T(1,128)}, u32[]{:S(2)}) copy-start(f32[1,3]{1,0:T(1,128)} %param.13) | copy-start | bytes 40
  40.5 184.3 %all-to-all-start = ((f32[64,1,1,2048]{3,2,1,0:T(1,128)}), f32[64,1,1,2048]{3,2,1,0:T(1,128)S(1)}, u32[]{:S(2)}, u32[]{:S(2)}) async-start(f32[64,1,1,2048]{3,2,1,0:T(1,128)} %stack.6), calls=%async_computation | async-start | bytes 1048576 | tf_op jit(solution)/shard_map/all_to_all | solution.py:58
  225.5 6.9 %collective-permute-start.3 = (f32[2,1,1,2048]{3,2,1,0:T(1,128)S(1)}, f32[2,1,1,2048]{3,2,1,0:T(1,128)S(1)}, u32[]{:S(2)}, u32[]{:S(2)}) collective-permute-start(f32[2,1,1,2048]{3,2,1,0:T(1,128)S(1)} %pad_maximum_fusion), channel_id=1, source_target_pairs={{1,0},{2,1},{3,2},{5,4},{6,5},{7,6},{9,8},{10,9},{11,10},{13,12},{... | collective-permute-start | bytes 49160 | tf_op jit(solution)/shard_map/ppermute | solution.py:17
  228.9 3.5 %collective-permute-start.2 = (f32[2,1,1,2048]{3,2,1,0:T(1,128)S(1)}, f32[2,1,1,2048]{3,2,1,0:T(1,128)S(1)}, u32[]{:S(2)}, u32[]{:S(2)}) collective-permute-start(f32[2,1,1,2048]{3,2,1,0:T(1,128)S(1)} %pad_maximum_fusion), channel_id=1, source_target_pairs={{0,1},{1,2},{2,3},{4,5},{5,6},{6,7},{8,9},{9,10},{10,11},{12,13},{... | collective-permute-start | bytes 49160 | tf_op jit(solution)/shard_map/ppermute | solution.py:14
